TPU v7x, 32 devices: a whole 2x2x4 slice. The times are simulated.
32 devices in a mesh: lat: 4 (over y, x), lon: 8 (over z, core).
Axes of the slice: x: 2, y: 2, z: 4, core: 2. Of those that a mesh axis runs over, the one named last changes fastest.
Arguments:
- base_state: float32 [8, 2, 480, 1024], P(None, None, 'lat', 'lon'), may hold values from -6 to 6
- section_state: float32 [8, 2, 480, 1024], P(None, None, 'lat', 'lon'), may hold values from -6 to 6
- cutoff: int32 [480], replicated, may hold values from 8 to 64, as said below
- filter_mask: int32 [480], replicated, may hold values from 0 to 1, as said below
Outputs:
- new_state: float32 [8, 2, 480, 1024], P(None, None, 'lat', 'lon')
Inputs may be any that keep to these rules, and one draw needn't show every extreme that they name: `cutoff`: every value lies in 8 to 64, and 64 occurs in every draw. `filter_mask`: 1 exactly on a run of rows starting at each pole, 0 elsewhere; each run holds 1 to 120 rows, and one of the two runs holds exactly 120.
All inputs are finite; a program needn't handle non-finite values.
Results may differ from a plain program's by a relative error of at most 0.0003.
Values sent between devices are 32-bit elements; how exact they have to be, the bound alone decides.
A program may use at most 64 MiB of HBM per device.

v0:
```python
import jax
import jax.numpy as jnp
from jax import lax
from jax.sharding import PartitionSpec as P

KMAX = 64


section_weight = 0.4


def passed_along(block, axis, distance):
    devices = range(lax.axis_size(axis))
    route = [((i - distance) % len(devices), i) for i in devices]
    return lax.ppermute(block, axis, route)


def padded_2(block, sides, width, periodic):
    for axis, dim in sides:
        count = lax.axis_size(axis)
        forward = [(i, i + 1) for i in range(count - 1)]
        if periodic:
            forward.append((count - 1, 0))
        backward = [(target, source) for source, target in forward]
        low = lax.ppermute(
            lax.slice_in_dim(block, block.shape[dim] - width, None, axis=dim), axis, forward
        )
        high = lax.ppermute(lax.slice_in_dim(block, 0, width, axis=dim), axis, backward)
        block = jnp.concatenate([low, block, high], axis=dim)
    return block


def interface(padded, along):
    length = padded.shape[along]
    outer_low = lax.slice_in_dim(padded, 0, length - 3, axis=along)
    inner_low = lax.slice_in_dim(padded, 1, length - 2, axis=along)
    inner_high = lax.slice_in_dim(padded, 2, length - 1, axis=along)
    outer_high = lax.slice_in_dim(padded, 3, length, axis=along)
    return (7.0 * (inner_low + inner_high) - (outer_low + outer_high)) / 12.0


def cell_cosine(first_row, row_count, total_rows):
    index_rows = first_row + jnp.arange(row_count, dtype=jnp.int32)
    return jnp.sin(jnp.pi * (index_rows.astype(jnp.float32) + 0.5) / total_rows)


def face_cosine(first_row, row_count, total_rows):
    index_faces = first_row + jnp.arange(row_count + 1, dtype=jnp.int32)
    raw_values = jnp.sin(jnp.pi * index_faces.astype(jnp.float32) / total_rows)
    return jnp.where((index_faces == 0) | (index_faces == total_rows), 0.0, raw_values)


def make_basis(positions, total_cols):
    product_index = positions[:, None] * jnp.arange(KMAX, dtype=jnp.int32)[None, :] % total_cols
    phases = product_index.astype(jnp.float32) * (2.0 * jnp.pi / total_cols)
    return jnp.concatenate([jnp.cos(phases), jnp.sin(phases)], axis=1)


def mode_scales(total_cols):
    mode_index = jnp.arange(2 * KMAX, dtype=jnp.int32) % KMAX
    mode_scale = jnp.where(mode_index == 0, 1.0 / total_cols, 2.0 / total_cols).astype(jnp.float32)
    return (mode_index.astype(jnp.float32), mode_scale)


def run_filter(row_values, cut_rows, total_cols):
    fields, levels, row_count, col_count = row_values.shape
    mode_index, mode_scale = mode_scales(total_cols)
    fourier_basis = make_basis(jnp.arange(total_cols, dtype=jnp.int32), total_cols)
    flattened = row_values.reshape(fields * levels * row_count, 1, col_count)
    cut_plane = jnp.broadcast_to(
        cut_rows.astype(jnp.float32)[None, :], (fields * levels, row_count)
    ).reshape(fields * levels * row_count, 1, 1)
    whole_rows = lax.all_to_all(flattened, "lon", split_axis=0, concat_axis=2, tiled=True)
    cut_values = lax.all_to_all(cut_plane, "lon", split_axis=0, concat_axis=2, tiled=True)
    weights = jnp.where(
        mode_index[None, None, :] < cut_values[..., :1], mode_scale[None, None, :], 0.0
    )
    coefficients = jnp.einsum(
        "arn,nk->ark", whole_rows, fourier_basis, precision=lax.Precision.HIGHEST
    )
    projected = jnp.einsum(
        "ark,nk->arn", coefficients * weights, fourier_basis, precision=lax.Precision.HIGHEST
    )
    result = lax.all_to_all(projected, "lon", split_axis=2, concat_axis=0, tiled=True)
    return result.reshape(fields, levels, row_count, col_count)


def local(base_state, section_state, cutoff, filter_mask):
    fields, levels, row_count, col_count = section_state.shape
    lat_count = lax.axis_size("lat")
    lon_count = lax.axis_size("lon")
    band_index = lax.axis_index("lat")
    total_rows = row_count * lat_count
    total_cols = col_count * lon_count
    first_row = band_index * row_count
    flip_sign = jnp.where(jnp.arange(fields) < 2, -1.0, 1.0).astype(jnp.float32)[:, None, None]
    polar_edge = jnp.where(
        band_index == 0, section_state[:, :, 0, :], section_state[:, :, row_count - 1, :]
    )
    crossed = passed_along(polar_edge, "lon", lon_count // 2) * flip_sign
    lat_padded = padded_2(section_state, (("lat", 2),), 2, False)
    south_row = jnp.where(band_index == 0, crossed, lat_padded[:, :, 1, :])
    north_row = jnp.where(band_index == lat_count - 1, crossed, lat_padded[:, :, row_count + 2, :])
    lat_padded = lat_padded.at[:, :, 1, :].set(south_row).at[:, :, row_count + 2, :].set(north_row)
    lon_padded = padded_2(section_state, (("lon", 3),), 2, True)
    face_cos = face_cosine(first_row, row_count, total_rows)
    cell_cos = cell_cosine(first_row, row_count, total_rows)
    lat_faces = interface(lat_padded, 2)
    lon_faces = interface(lon_padded, 3)
    north_flux = lat_faces[1][None] * lat_faces * face_cos[None, None, :, None]
    east_flux = lon_faces[0][None] * lon_faces
    tendency = (
        -(east_flux[..., 1:] - east_flux[..., :-1] + (north_flux[:, :, 1:] - north_flux[:, :, :-1]))
        / cell_cos[None, None, :, None]
    )
    own_mask = lax.dynamic_slice_in_dim(filter_mask, first_row, row_count)
    cut_rows = lax.dynamic_slice_in_dim(cutoff, first_row, row_count)
    smooth = run_filter(tendency, cut_rows, total_cols)
    filtered = jnp.where(own_mask[None, None, :, None] == 1, smooth, tendency)
    return base_state + section_weight * filtered


def solution(mesh):
    placed = (P(None, None, "lat", "lon"), P(None, None, "lat", "lon"), P(), P())
    return jax.shard_map(
        local, mesh=mesh, in_specs=placed, out_specs=P(None, None, "lat", "lon"), check_vma=False
    )
```

profile of v0, /device:TPU:0, one launch (start us, length us, event | category | flops | bytes accessed | tf_op | source)
XLA Modules:
  0.0 114.5 jit_solution(8694511773537524980)
XLA Ops:
  0.0 0.9 fusion.28
  0.9 4.1 %collective-permute-start.4 = (f32[8,2,128]{2,1,0:T(2,128)S(1)}, f32[8,2,128]{2,1,0:T(2,128)S(1)}, u32[]{:S(2)}, u32[]{:S(2)}) collective-permute-start(f32[8,2,128]{2,1,0:T(2,128)S(1)} %select_bitcast_fusion), channel_id=1, source_target_pairs={{4,0},{5,1},{6,2},{7,3},{0,4},{1,5},{2,6},{3,7},{12,8},{13,9},{14,... | collective-permute-start | bytes 24584 | tf_op jit(solution)/shard_map/ppermute | solution.py:15
  5.0 0.9 fusion.29
  5.9 3.4 %collective-permute-start.2 = (f32[8,2,2,128]{3,1,0,2:T(2,128)S(1)}, f32[8,2,2,128]{3,1,0,2:T(2,128)S(1)}, u32[]{:S(2)}, u32[]{:S(2)}) collective-permute-start(f32[8,2,2,128]{3,1,0,2:T(2,128)S(1)} %copy.76), channel_id=1, source_target_pairs={{0,8},{8,16},{16,24},{1,9},{9,17},{17,25},{2,10},{10,18},{18,26},{... | collective-permute-start | bytes 49160 | tf_op jit(solution)/shard_map/ppermute | solution.py:25
  9.3 1.3 %collective-permute-start.3 = (f32[8,2,2,128]{3,1,0,2:T(2,128)S(1)}, f32[8,2,2,128]{3,1,0,2:T(2,128)S(1)}, u32[]{:S(2)}, u32[]{:S(2)}) collective-permute-start(f32[8,2,2,128]{3,1,0,2:T(2,128)S(1)} %copy.77), channel_id=1, source_target_pairs={{8,0},{16,8},{24,16},{9,1},{17,9},{25,17},{10,2},{18,10},{26,18},{... | collective-permute-start | bytes 49160 | tf_op jit(solution)/shard_map/ppermute | solution.py:28
  10.6 2.1 %fusion.27 = (f32[8,2,120,2]{3,2,1,0:T(8,128)S(1)}, f32[8,2,120,2]{3,2,1,0:T(8,128)S(1)}) fusion(f32[8,2,120,128]{3,2,1,0:T(8,128)} %param.9), kind=kLoop, calls=%fused_computation.56 | loop fusion | bytes 61440 | tf_op jit(solution)/shard_map/slice | solution.py:26
  12.7 0.3 copy.74
  13.0 0.0 collective-permute-start
  13.1 0.3 copy.75
  13.4 3.6 %collective-permute-start.1 = (f32[8,2,120,2]{2,0,3,1:T(8,128)S(1)}, f32[8,2,120,2]{2,0,3,1:T(8,128)S(1)}, u32[]{:S(2)}, u32[]{:S(2)}) collective-permute-start(f32[8,2,120,2]{2,0,3,1:T(8,128)S(1)} %copy.75), channel_id=1, source_target_pairs={{1,0},{2,1},{3,2},{4,3},{5,4},{6,5},{7,6},{0,7},{9,8},{10,9},{11,1... | collective-permute-start | bytes 46088 | tf_op jit(solution)/shard_map/ppermute | solution.py:28
  16.9 0.8 dynamic-slice_convert_fusion
  17.7 1.6 %reshape.151 = f32[1920,1,1]{2,1,0:T(1,128)S(1)} reshape(f32[16,120]{1,0:T(8,128)S(1)} %broadcast_in_dim.58) | data formatting | bytes 15360 | tf_op jit(solution)/shard_map/reshape | solution.py:72
  19.2 0.6 broadcast.163
  19.8 14.9 %reduce.5 = f32[1920]{0:T(1024)S(1)} reduce(f32[1920,1,1]{2,1,0:T(1,128)S(1)} %reshape.151, f32[]{:T(128)} %broadcast.163), dimensions={1,2}, to_apply=%reshape.151.reduce_sub_computation | reduce | bytes 15364 | tf_op jit(solution)/shard_map/reshape | solution.py:72
  34.7 0.7 reshape.153
  35.4 3.3 %all-to-all-start.1 = ((f32[8,1,240]{2,1,0:T(1,128)}), f32[8,1,240]{2,1,0:T(1,128)S(1)}, u32[]{:S(2)}, u32[]{:S(2)}) async-start(f32[8,1,240]{2,1,0:T(1,128)} %reshape.153), calls=%async_computation.1 | async-start | bytes 16384 | tf_op jit(solution)/shard_map/all_to_all | solution.py:74
  38.8 0.0 collective-permute-done
  38.8 0.3 copy.60
  39.2 0.0 collective-permute-done.1
  39.2 0.3 copy.62
  39.5 2.1 %fusion.1 = f32[8,2,120,129]{3,2,1,0:T(8,128)S(1)} fusion(f32[8,2,120,2]{3,2,1,0:T(8,128)S(1)} %copy.62, f32[8,2,120,128]{3,2,1,0:T(8,128)S(1)} %copy-done, f32[8,2,120,2]{3,2,1,0:T(8,128)S(1)} %copy.60), kind=kLoop, calls=%fused_computation.2 | loop fusion | flops 1981440 | bytes 2004480 | tf_op jit(solution)/shard_map/sub | solution.py:39
  41.7 1.4 %broadcast_multiply_fusion = f32[8,2,120,129]{3,2,1,0:T(8,128)} fusion(f32[8,2,120,129]{3,2,1,0:T(8,128)S(1)} %fusion.1, f32[2,120,129]{2,1,0:T(8,128)S(1)} %fusion.19), kind=kLoop, calls=%fused_computation.22 | loop fusion | flops 247680 | bytes 2105280 | tf_op jit(solution)/shard_map/mul | solution.py:111
  43.1 0.0 collective-permute-done.2
  43.1 0.0 collective-permute-done.3
  43.2 0.1 pad_maximum_fusion.2
  43.3 0.1 fusion.22
  43.4 0.1 scatter.9
  43.5 0.3 fusion.3
  43.9 0.4 multiply_multiply_fusion
  44.3 1.1 copy-done.1
  45.4 1.3 %fusion.9 = f32[8,2,120,128]{3,2,1,0:T(8,128)} fusion(f32[8,2,121,128]{3,2,1,0:T(8,128)S(1)} %multiply_multiply_fusion, f32[8,2,120,129]{3,2,1,0:T(8,128)S(1)} %copy-done.1, f32[120]{0:T(128)S(1)} %multiply_sine_fusion), kind=kLoop, calls=%fused_computation.19 | loop fusion | flops 1228800 | bytes 4915680 | tf_op jit(solution)/shard_map/div | solution.py:113
  46.7 0.0 all-to-all-done.1
  46.7 5.0 %all-to-all-start = ((f32[1920,1,128]{2,1,0:T(1,128)}), f32[1920,1,128]{2,1,0:T(1,128)S(1)}, u32[]{:S(2)}, u32[]{:S(2)}) async-start(f32[1920,1,128]{2,1,0:T(1,128)} %bitcast.8), calls=%async_computation | async-start | bytes 1966080 | tf_op jit(solution)/shard_map/all_to_all | solution.py:73
  51.8 2.1 %fusion.16 = (f32[1024,64]{1,0:T(8,128)S(1)}, f32[1024,64]{1,0:T(8,128)S(1)}) fusion(), kind=kLoop, calls=%fused_computation.33 | loop fusion | flops 917504 | bytes 524288 | tf_op jit(solution)/shard_map/sin | solution.py:56
  53.8 0.6 reduce.6
  54.5 1.6 %reshape.154 = f32[1920,1,1]{2,1,0:T(1,128)S(1)} reshape(f32[8,240]{1,0:T(8,128)S(1)} %reduce.6) | data formatting | bytes 15360
  56.0 14.3 %reduce.4 = f32[1920]{0:T(1024)S(1)} reduce(f32[1920,1,1]{2,1,0:T(1,128)S(1)} %reshape.154, f32[]{:T(128)} %constant.137), dimensions={1,2}, to_apply=%all_to_all.38.reduce_sub_computation | reduce | bytes 15364 | tf_op jit(solution)/shard_map/all_to_all | solution.py:74
  70.3 0.1 all_to_all.39
  70.4 6.5 %all-to-all-done = f32[1920,1,128]{2,1,0:T(1,128)S(1)} async-done(((f32[1920,1,128]{2,1,0:T(1,128)}), f32[1920,1,128]{2,1,0:T(1,128)S(1)}, u32[]{:S(2)}, u32[]{:S(2)}) %all-to-all-start) | async-done | bytes 983072 | tf_op jit(solution)/shard_map/all_to_all | solution.py:73
  76.9 0.3 copy.70
  77.2 1.1 convolution_multiply_fusion
  78.3 1.1 convolution_bitcast_fusion
  79.4 1.9 %copy.72 = f32[240,1,1024]{0,1,2:T(1,128)} copy(f32[240,1,1024]{2,0,1:T(8,128)S(1)} %convolution_bitcast_fusion) | data formatting | bytes 1966080 | tf_op jit(solution)/shard_map/ark,nk->arn/dot_general | solution.py:81
  81.3 3.7 %all-to-all-start.2 = ((f32[240,1,1024]{0,1,2:T(1,128)}), f32[240,1,1024]{0,1,2:T(1,128)S(1)}, u32[]{:S(2)}, u32[]{:S(2)}) async-start(f32[240,1,1024]{0,1,2:T(1,128)} %copy.72), calls=%async_computation.2 | async-start | bytes 2097152 | tf_op jit(solution)/shard_map/all_to_all | solution.py:84
  85.0 0.8 dynamic-slice_compare_fusion
  85.8 25.8 %all-to-all-done.2 = f32[240,1,1024]{0,1,2:T(1,128)S(1)} async-done(((f32[240,1,1024]{0,1,2:T(1,128)}), f32[240,1,1024]{0,1,2:T(1,128)S(1)}, u32[]{:S(2)}, u32[]{:S(2)}) %all-to-all-start.2) | async-done | bytes 983072 | tf_op jit(solution)/shard_map/all_to_all | solution.py:84
  111.5 0.6 copy.73
  112.2 2.4 %multiply_add_fusion = f32[8,2,120,128]{3,2,1,0:T(8,128)} fusion(f32[8,2,120,128]{3,2,1,0:T(8,128)S(1)} %copy-done.2, f32[8,2,120,128]{3,2,1,0:T(8,128)S(1)} %bitcast.44, f32[8,2,120,128]{3,2,1,0:T(8,128)} %fusion.9, pred[120]{0:T(512)(128)(4,1)S(1)} %dynamic-slice_compare_fusion), kind=kLoop, calls=%fused_computation.21 | loop fusion | flops 737280 | bytes 3932280 | tf_op jit(solution)/shard_map/add | solution.py:120
  (21 shorter events, 0.3 us)
Async XLA Ops:
  0.9 42.4 %collective-permute-start.4 = (f32[8,2,128]{2,1,0:T(2,128)S(1)}, f32[8,2,128]{2,1,0:T(2,128)S(1)}, u32[]{:S(2)}, u32[]{:S(2)}) collective-permute-start(f32[8,2,128]{2,1,0:T(2,128)S(1)} %select_bitcast_fusion), channel_id=1, source_target_pairs={{4,0},{5,1},{6,2},{7,3},{0,4},{1,5},{2,6},{3,7},{12,8},{13,9},{14,... | collective-permute-start | bytes 24584 | tf_op jit(solution)/shard_map/ppermute | solution.py:15
  5.9 37.2 %collective-permute-start.2 = (f32[8,2,2,128]{3,1,0,2:T(2,128)S(1)}, f32[8,2,2,128]{3,1,0,2:T(2,128)S(1)}, u32[]{:S(2)}, u32[]{:S(2)}) collective-permute-start(f32[8,2,2,128]{3,1,0,2:T(2,128)S(1)} %copy.76), channel_id=1, source_target_pairs={{0,8},{8,16},{16,24},{1,9},{9,17},{17,25},{2,10},{10,18},{18,26},{... | collective-permute-start | bytes 49160 | tf_op jit(solution)/shard_map/ppermute | solution.py:25
  9.3 33.8 %collective-permute-start.3 = (f32[8,2,2,128]{3,1,0,2:T(2,128)S(1)}, f32[8,2,2,128]{3,1,0,2:T(2,128)S(1)}, u32[]{:S(2)}, u32[]{:S(2)}) collective-permute-start(f32[8,2,2,128]{3,1,0,2:T(2,128)S(1)} %copy.77), channel_id=1, source_target_pairs={{8,0},{16,8},{24,16},{9,1},{17,9},{25,17},{10,2},{18,10},{26,18},{... | collective-permute-start | bytes 49160 | tf_op jit(solution)/shard_map/ppermute | solution.py:28
  13.0 25.8 %collective-permute-start = (f32[8,2,120,2]{2,0,3,1:T(8,128)S(1)}, f32[8,2,120,2]{2,0,3,1:T(8,128)S(1)}, u32[]{:S(2)}, u32[]{:S(2)}) collective-permute-start(f32[8,2,120,2]{2,0,3,1:T(8,128)S(1)} %copy.74), channel_id=1, source_target_pairs={{0,1},{1,2},{2,3},{3,4},{4,5},{5,6},{6,7},{7,0},{8,9},{9,10},{10,1... | collective-permute-start | bytes 46088 | tf_op jit(solution)/shard_map/ppermute | solution.py:25
  13.4 25.8 %collective-permute-start.1 = (f32[8,2,120,2]{2,0,3,1:T(8,128)S(1)}, f32[8,2,120,2]{2,0,3,1:T(8,128)S(1)}, u32[]{:S(2)}, u32[]{:S(2)}) collective-permute-start(f32[8,2,120,2]{2,0,3,1:T(8,128)S(1)} %copy.75), channel_id=1, source_target_pairs={{1,0},{2,1},{3,2},{4,3},{5,4},{6,5},{7,6},{0,7},{9,8},{10,9},{11,1... | collective-permute-start | bytes 46088 | tf_op jit(solution)/shard_map/ppermute | solution.py:28
  17.7 21.9 %copy-start = (f32[8,2,120,128]{3,2,1,0:T(8,128)S(1)}, f32[8,2,120,128]{3,2,1,0:T(8,128)}, u32[]{:S(2)}) copy-start(f32[8,2,120,128]{3,2,1,0:T(8,128)} %param.9) | copy-start | bytes 2949124
  35.4 11.3 %all-to-all-start.1 = ((f32[8,1,240]{2,1,0:T(1,128)}), f32[8,1,240]{2,1,0:T(1,128)S(1)}, u32[]{:S(2)}, u32[]{:S(2)}) async-start(f32[8,1,240]{2,1,0:T(1,128)} %reshape.153), calls=%async_computation.1 | async-start | bytes 16384 | tf_op jit(solution)/shard_map/all_to_all | solution.py:74
  43.9 1.5 %copy-start.1 = (f32[8,2,120,129]{3,2,1,0:T(8,128)S(1)}, f32[8,2,120,129]{3,2,1,0:T(8,128)}, u32[]{:S(2)}) copy-start(f32[8,2,120,129]{3,2,1,0:T(8,128)} %broadcast_multiply_fusion) | copy-start | bytes 2972164
  46.7 30.2 %all-to-all-start = ((f32[1920,1,128]{2,1,0:T(1,128)}), f32[1920,1,128]{2,1,0:T(1,128)S(1)}, u32[]{:S(2)}, u32[]{:S(2)}) async-start(f32[1920,1,128]{2,1,0:T(1,128)} %bitcast.8), calls=%async_computation | async-start | bytes 1966080 | tf_op jit(solution)/shard_map/all_to_all | solution.py:73
  81.3 30.9 %copy-start.2 = (f32[8,2,120,128]{3,2,1,0:T(8,128)S(1)}, f32[8,2,120,128]{3,2,1,0:T(8,128)}, u32[]{:S(2)}) copy-start(f32[8,2,120,128]{3,2,1,0:T(8,128)} %param.8) | copy-start | bytes 2949124
  81.3 30.2 %all-to-all-start.2 = ((f32[240,1,1024]{0,1,2:T(1,128)}), f32[240,1,1024]{0,1,2:T(1,128)S(1)}, u32[]{:S(2)}, u32[]{:S(2)}) async-start(f32[240,1,1024]{0,1,2:T(1,128)} %copy.72), calls=%async_computation.2 | async-start | bytes 2097152 | tf_op jit(solution)/shard_map/all_to_all | solution.py:84
where the time goes:
time: 116 us; the launch traced here: 115 us
  other arithmetic  41.7 us (36%)
  waiting for transfers between devices  32.3 us (28%)
  starting transfers between devices  24.4 us (21%)
  local copies, waits for them, and re-layouts  13.7 us (12%)
  matrix products  2.14 us (2%)
    all_to_all x1, waiting for transfers between devices, run_filter(): lax.all_to_all(projected, 'lon', split_axis=2, concat_axis=0, tiled=True)  25.8 us
    all_to_all x2, other arithmetic, run_filter(): lax.all_to_all(cut_plane, 'lon', split_axis=0, concat_axis=2, tiled=True)  14.9 us
    reshape x1, other arithmetic, run_filter(): cut_plane = jnp.broadcast_to(cut_rows.astype(jnp.float32)[None, :], (fiel...  14.9 us
    all_to_all x1, waiting for transfers between devices, run_filter(): lax.all_to_all(flattened, 'lon', split_axis=0, concat_axis=2, tiled=True)  6.49 us
    all_to_all x1, starting transfers between devices, run_filter(): lax.all_to_all(flattened, 'lon', split_axis=0, concat_axis=2, tiled=True)  5.02 us
    ppermute x2, starting transfers between devices, padded_2(): lax.ppermute(lax.slice_in_dim(block, 0, width, axis=dim), axis, backward)  4.85 us
    ppermute x1, starting transfers between devices, passed_along(): return lax.ppermute(block, axis, route)  4.1 us
    unnamed x12, local copies, waits for them, and re-layouts  3.99 us
  transfers between devices with their start and end apart: 8, of which 2 were waited for; matrix products, arithmetic and copies ran while one was open for 42% of the time, Pallas kernels for 0%

commit v1 on v0

v1 whole, which is shorter than its diff:
```python
import functools

import jax
import jax.numpy as jnp
import ml_dtypes
import numpy as np
from jax import lax
from jax.experimental import pallas as pl
from jax.experimental.pallas import tpu as pltpu
from jax.sharding import PartitionSpec as P

KMAX = 64
MODES = 2 * KMAX
LANES = 128
section_weight = 0.4
MESH = pl.DeviceIdType.MESH


def split_halves(table):
    high = table.astype(ml_dtypes.bfloat16)
    low = (table - high.astype(np.float64)).astype(ml_dtypes.bfloat16)
    return high, low


def basis_tables(lon_count, cols):
    total = lon_count * cols
    phase = (np.arange(total)[:, None] * np.arange(KMAX)[None, :]) % total * (2.0 * np.pi / total)
    basis = np.concatenate([np.cos(phase), np.sin(phase)], axis=1).reshape(lon_count, cols, MODES)
    high, low = split_halves(basis)
    wide = np.concatenate([high, low], axis=2)
    forward = np.concatenate([wide, wide], axis=1)
    tall = np.concatenate([high.transpose(0, 2, 1), low.transpose(0, 2, 1)], axis=2)
    inverse = np.concatenate([tall, tall], axis=1)
    return forward, inverse


def geometry_table(lat_count, rows, cols):
    total = lat_count * rows
    faces = np.arange(lat_count)[:, None] * rows + np.arange(rows + 8)[None, :]
    face = np.where((faces == 0) | (faces >= total), 0.0, np.sin(np.pi * faces / total))
    cell = -1.0 / (144.0 * np.sin(np.pi * (np.minimum(faces, total - 1) + 0.5) / total))
    both = np.stack([face, cell], axis=1).astype(np.float32)
    return np.ascontiguousarray(np.broadcast_to(both[..., None], both.shape + (cols,)))


def two_parts(value):
    high = value.astype(jnp.bfloat16)
    low = (value - high.astype(jnp.float32)).astype(jnp.bfloat16)
    return jnp.concatenate([high, low], axis=1)


def kernel(dims, base_hbm, sec_hbm, cut_ref, mask_ref, fwd_hbm, inv_hbm, geo_hbm, out_ref,
           pad, base, fwd, inv, geo, wts, msk, rowpack, halo, colpack, colrecv, comb, ul, ur, vf,
           tend, msend, mrecv, zsend, zrecv, coef,
           lsem, hs_sem, hr_sem, ms_sem, mr_sem, zs_sem, zr_sem, cs_sem, cr_sem, fs_sem):
    F, L, R, C, NLAT, NLON = dims
    S = F * L
    G = NLON // 2
    FG = F // G
    quarter = -(-NLAT // 4)
    band = lax.axis_index("lat")
    lon = lax.axis_index("lon")
    core = lax.rem(lon, 2)
    g = lon // 2
    mate = g * 2 + 1 - core
    polar = (band < quarter) | (band >= NLAT - quarter)

    locals_ = [
        pltpu.make_async_copy(sec_hbm, pad.at[:, pl.ds(8, R), :], lsem.at[0]),
        pltpu.make_async_copy(base_hbm, base, lsem.at[1]),
        pltpu.make_async_copy(fwd_hbm.at[lon], fwd, lsem.at[2]),
        pltpu.make_async_copy(inv_hbm.at[lon], inv, lsem.at[3]),
        pltpu.make_async_copy(geo_hbm.at[band], geo, lsem.at[4]),
    ]
    for copy in locals_:
        copy.start()

    left = lax.rem(lon + NLON - 1, NLON)
    right = lax.rem(lon + 1, NLON)
    cross = lax.rem(lon + NLON // 2, NLON)
    south, north = band == 0, band == NLAT - 1
    lo_dst = (jnp.where(south, 0, band - 1), jnp.where(south, cross, lon))
    hi_dst = (jnp.where(north, band, band + 1), jnp.where(north, cross, lon))
    lo_slot = jnp.where(south, 0, 1)
    hi_slot = jnp.where(north, 1, 0)

    def peer(d):
        return lax.rem(g + d, G)

    barrier = pltpu.get_barrier_semaphore()
    for target in ((band, left), (band, right), lo_dst, hi_dst):
        pl.semaphore_signal(barrier, inc=1, device_id=target, device_id_type=MESH)

    @pl.when(polar)
    def _():
        for d in range(1, G):
            pl.semaphore_signal(
                barrier, inc=1, device_id=(band, peer(d) * 2 + core), device_id_type=MESH
            )

    locals_[0].wait()
    lane = lax.broadcasted_iota(jnp.int32, (R, LANES), 1)
    packed = jnp.zeros((R, LANES), jnp.float32)
    for s in range(S):
        rowpack[0, 2 * s : 2 * s + 2] = pad[s, 8:10]
        rowpack[1, 2 * s : 2 * s + 2] = pad[s, R + 6 : R + 8]
        edge = pad[s, 8 : R + 8, 0:LANES]
        if C > LANES:
            edge = jnp.where(lane < LANES // 2, edge, pad[s, 8 : R + 8, C - LANES : C])
        shifted = pltpu.roll(edge, (4 * s + 2) % LANES, 1)
        packed = jnp.where((lane >= 4 * s) & (lane < 4 * s + 4), shifted, packed)
    colpack[...] = packed

    pl.semaphore_wait(barrier, jnp.where(polar, G + 3, 4))

    def remote(src, dst, send, recv, target):
        return pltpu.make_async_remote_copy(
            src_ref=src, dst_ref=dst, send_sem=send, recv_sem=recv, device_id=target, device_id_type=MESH
        )

    halos = [
        remote(colpack, colrecv.at[0], hs_sem.at[0], hr_sem.at[0], (band, right)),
        remote(colpack, colrecv.at[1], hs_sem.at[1], hr_sem.at[1], (band, left)),
        remote(rowpack.at[0], halo.at[lo_slot], hs_sem.at[2], hr_sem.at[2 + lo_slot], lo_dst),
        remote(rowpack.at[1], halo.at[hi_slot], hs_sem.at[3], hr_sem.at[2 + hi_slot], hi_dst),
    ]
    for copy in halos:
        copy.start()

    @pl.when(polar)
    def _():
        mode = lax.rem(lax.broadcasted_iota(jnp.int32, (1, MODES), 1), KMAX)
        scale = jnp.where(mode == 0, 1.0 / (C * NLON), 2.0 / (C * NLON)).astype(jnp.float32)

        def row(r, carry):
            wts[pl.ds(r, 1), :] = jnp.where(mode < cut_ref[band * R + r], scale, 0.0)
            msk[pl.ds(r, 1), :] = jnp.broadcast_to(mask_ref[band * R + r], (1, C))
            return carry

        lax.fori_loop(0, R, row, 0)

    for copy in locals_[1:]:
        copy.wait()
    for slot in range(2):
        remote(colpack, colrecv.at[slot], hs_sem.at[slot], hr_sem.at[slot], (band, right)).wait_recv()
        remote(
            rowpack.at[slot], halo.at[slot], hs_sem.at[2 + slot], hr_sem.at[2 + slot], (band, right)
        ).wait_recv()

    comb[...] = jnp.where(lax.rem(lane, 4) < 2, colrecv[0], colrecv[1])
    index = lax.broadcasted_iota(jnp.int32, (2 * S, C), 0)
    sign = jnp.where(index < 4 * L, -1.0, 1.0)
    low, high = halo[0], halo[1]
    over_low = jnp.where(lax.rem(index, 2) == 1, sign * pltpu.roll(low, 1, 0), 0.0)
    over_high = jnp.where(lax.rem(index, 2) == 0, sign * pltpu.roll(high, 2 * S - 1, 0), 0.0)
    low = jnp.where(south, over_low, low)
    high = jnp.where(north, over_high, high)
    for s in range(S):
        pad[s, 6:8] = low[2 * s : 2 * s + 2]
        pad[s, R + 8 : R + 10] = high[2 * s : 2 * s + 2]

    wide = lax.broadcasted_iota(jnp.int32, (R, C), 1)

    def east(s):
        x = pad[s, 8 : R + 8]
        e = pltpu.roll(comb[...], lax.rem(2 * LANES - 2 - 4 * s, LANES), 1)
        if C > LANES:
            e = jnp.concatenate([e] * (C // LANES), axis=1)
        m1 = pltpu.roll(jnp.where(wide == C - 1, e, x), 1, 1)
        m2 = pltpu.roll(jnp.where(wide >= C - 2, e, x), 2, 1)
        p1 = pltpu.roll(jnp.where(wide == 0, e, x), C - 1, 1)
        p2 = pltpu.roll(jnp.where(wide < 2, e, x), C - 2, 1)
        return 7.0 * (m1 + x) - (m2 + p1), 7.0 * (x + p1) - (m1 + p2)

    def northward(s):
        return 7.0 * (pad[s, 7 : R + 15] + pad[s, 8 : R + 16]) - (pad[s, 6 : R + 14] + pad[s, 9 : R + 17])

    def winds(l):
        ul[...], ur[...] = east(l)
        vf[...] = northward(L + l) * geo[0]

    def tendency(s):
        wl, wr = east(s)
        fn = vf[...] * northward(s)
        up = pltpu.roll(fn, R + 7, 0)
        return ((ur[...] * wr - ul[...] * wl) + (up[:R] - fn[:R])) * geo[1, :R]

    @pl.when(jnp.logical_not(polar))
    def _():
        def level(l, carry):
            winds(l)

            def field(f, inner):
                s = f * L + l
                out_ref[s] = base[s] + section_weight * tendency(s)
                return inner

            return lax.fori_loop(0, F, field, carry)

        lax.fori_loop(0, L, level, 0)

    @pl.when(polar)
    def _():
        here, other = core, 1 - core

        def order(k):
            return lax.rem((g + 1) * FG + k, F)

        def partial_sums(f, l):
            s = f * L + l
            t = tendency(s)
            tend[s] = t
            both = jnp.dot(two_parts(t), fwd[...], preferred_element_type=jnp.float32)
            return both[:, :MODES] + both[:, MODES:]

        def to_mate(f):
            return remote(msend.at[f], mrecv.at[f], ms_sem.at[f], mr_sem.at[f], (band, mate))

        def to_owner(f):
            slot = lax.rem(f, FG)
            return remote(
                zsend.at[f], zrecv.at[g * FG + slot], zs_sem.at[f], zr_sem.at[g * FG + slot],
                (band, (f // FG) * 2 + core),
            )

        def to_peer(f, d):
            at = here * F + f
            return remote(
                coef.at[at], coef.at[at], cs_sem.at[lax.rem(f, FG) * G + d], cr_sem.at[at],
                (band, peer(d) * 2 + core),
            )

        def forward(f):
            at = here * F + f
            return remote(coef.at[at], coef.at[at], fs_sem.at[f], cr_sem.at[at], (band, mate))

        def arrived(at):
            return remote(coef.at[at], coef.at[at], fs_sem.at[0], cr_sem.at[at], (band, mate))

        def finish(f, l):
            s = f * L + l
            both = jnp.dot(two_parts(coef[l * F + f]), inv[...], preferred_element_type=jnp.float32)
            smooth = both[:, :C] + both[:, C:]
            filtered = jnp.where(msk[...] == 1, smooth, tend[s])
            out_ref[s] = base[s] + section_weight * filtered

        winds(other)

        def stage_a(k, carry):
            f = order(k)
            msend[f] = partial_sums(f, other)
            to_mate(f).start()
            return carry

        lax.fori_loop(0, F, stage_a, 0)
        winds(here)

        def stage_b(k, carry):
            f = order(k)
            mine = partial_sums(f, here)
            to_mate(f).wait_recv()
            zsend[f] = mine + mrecv[f]

            @pl.when(k < F - FG)
            def _():
                to_owner(f).start()

            return carry

        lax.fori_loop(0, F, stage_b, 0)

        def stage_c(j, carry):
            f = g * FG + j
            total = zsend[f]
            for d in range(1, G):
                at = peer(d) * FG + j
                remote(zsend.at[f], zrecv.at[at], zs_sem.at[f], zr_sem.at[at], (band, mate)).wait_recv()
                total = total + zrecv[at]
            coef[here * F + f] = total * wts[...]
            for d in range(1, G):
                to_peer(f, d).start()
            forward(f).start()
            return carry

        lax.fori_loop(0, FG, stage_c, 0)

        def own(j, carry):
            finish(g * FG + j, here)
            return carry

        lax.fori_loop(0, FG, own, 0)

        def stage_d(k, carry):
            f = order(k)
            arrived(here * F + f).wait_recv()
            forward(f).start()
            finish(f, here)
            return carry

        lax.fori_loop(0, F - FG, stage_d, 0)

        def stage_e(k, carry):
            f = lax.rem(g * FG + k, F)
            arrived(other * F + f).wait_recv()
            finish(f, other)
            return carry

        lax.fori_loop(0, F, stage_e, 0)

        def drain(k, carry):
            f = order(k)
            to_mate(f).wait_send()
            forward(f).wait_send()

            @pl.when(k < F - FG)
            def _():
                to_owner(f).wait_send()

            return carry

        lax.fori_loop(0, F, drain, 0)

        def drain_peers(j, carry):
            for d in range(1, G):
                to_peer(g * FG + j, d).wait_send()
            return carry

        lax.fori_loop(0, FG, drain_peers, 0)

    for copy in halos:
        copy.wait_send()


def local(base_state, section_state, cutoff, filter_mask):
    F, L, R, C = section_state.shape
    NLAT, NLON = lax.axis_size("lat"), lax.axis_size("lon")
    S, G = F * L, NLON // 2
    FG = F // G
    forward, inverse = basis_tables(NLON, C)
    geometry = geometry_table(NLAT, R, C)
    f32 = jnp.float32
    sem = pltpu.SemaphoreType.DMA
    hbm = pl.BlockSpec(memory_space=pl.ANY)
    smem = pl.BlockSpec(memory_space=pltpu.SMEM)
    result = pl.pallas_call(
        functools.partial(kernel, (F, L, R, C, NLAT, NLON)),
        out_shape=jax.ShapeDtypeStruct((S, R, C), f32),
        in_specs=[hbm, hbm, smem, smem, hbm, hbm, hbm],
        out_specs=pl.BlockSpec(memory_space=pltpu.VMEM),
        scratch_shapes=[
            pltpu.VMEM((S, R + 24, C), f32),
            pltpu.VMEM((S, R, C), f32),
            pltpu.VMEM((2 * C, 2 * MODES), jnp.bfloat16),
            pltpu.VMEM((2 * MODES, 2 * C), jnp.bfloat16),
            pltpu.VMEM((2, R + 8, C), f32),
            pltpu.VMEM((R, MODES), f32),
            pltpu.VMEM((R, C), jnp.int32),
            pltpu.VMEM((2, 2 * S, C), f32),
            pltpu.VMEM((2, 2 * S, C), f32),
            pltpu.VMEM((R, LANES), f32),
            pltpu.VMEM((2, R, LANES), f32),
            pltpu.VMEM((R, LANES), f32),
            pltpu.VMEM((R, C), f32),
            pltpu.VMEM((R, C), f32),
            pltpu.VMEM((R + 8, C), f32),
            pltpu.VMEM((S, R, C), f32),
            pltpu.VMEM((F, R, MODES), f32),
            pltpu.VMEM((F, R, MODES), f32),
            pltpu.VMEM((F, R, MODES), f32),
            pltpu.VMEM((F, R, MODES), f32),
            pltpu.VMEM((S, R, MODES), f32),
            sem((5,)), sem((4,)), sem((4,)), sem((F,)), sem((F,)), sem((F,)), sem((F,)),
            sem((FG * G,)), sem((S,)), sem((F,)),
        ],
        compiler_params=pltpu.CompilerParams(
            collective_id=0, has_side_effects=True, vmem_limit_bytes=56 * 1024 * 1024
        ),
    )(
        base_state.reshape(S, R, C), section_state.reshape(S, R, C), cutoff, filter_mask,
        jnp.asarray(forward), jnp.asarray(inverse), jnp.asarray(geometry),
    )
    return result.reshape(F, L, R, C)


def solution(mesh):
    placed = (P(None, None, "lat", "lon"), P(None, None, "lat", "lon"), P(), P())
    return jax.shard_map(
        local, mesh=mesh, in_specs=placed, out_specs=P(None, None, "lat", "lon"), check_vma=False
    )
```

time: 116 us -> 41.5 us (0.36); the launches traced: 115 us -> 41.3 us
  other arithmetic: 41.7 us -> 0 us
  Pallas kernels: 0 us -> 39.1 us
  waiting for transfers between devices: 32.3 us -> 0 us
  starting transfers between devices: 24.4 us -> 0 us
  local copies, waits for them, and re-layouts: 13.7 us -> 2.21 us
  matrix products: 2.14 us -> 0 us
    pallas_call x0 -> x1, Pallas kernels: none -> 39.1 us  [local(): pl.pallas_call(functools.partial(kernel, (F, L, R, C, NLAT, NLON)), out_s...]
    all_to_all x3 -> x0, waiting for transfers between devices: 32.2 us -> none  [the longest x1 25.8 us: run_filter(): lax.all_to_all(projected, 'lon', split_axis=2, concat_axis=0, tiled=True)]
    all_to_all x2 -> x0, other arithmetic: 14.9 us -> none  [run_filter(): lax.all_to_all(cut_plane, 'lon', split_axis=0, concat_axis=2, tiled=True)]
    reshape x1 -> x0, other arithmetic: 14.9 us -> none  [run_filter(): cut_plane = jnp.broadcast_to(cut_rows.astype(jnp.float32)[None, :], (fiel...]
    ppermute x5 -> x0, starting transfers between devices: 12.4 us -> none  [the longest x2 4.85 us: padded_2(): lax.ppermute(lax.slice_in_dim(block, 0, width, axis=dim), axis, backward)]
    all_to_all x3 -> x0, starting transfers between devices: 12 us -> none  [the longest x1 5.02 us: run_filter(): lax.all_to_all(flattened, 'lon', split_axis=0, concat_axis=2, tiled=True)]
    slice x4 -> x0, local copies, waits for them, and re-layouts: 3.84 us -> none  [the longest x2 2.96 us: padded_2(): lax.slice_in_dim(block, block.shape[dim] - width, None, axis=dim)]
    sub x2 -> x0, other arithmetic: 2.43 us -> none  [interface(): return (7.0 * (inner_low + inner_high) - (outer_low + outer_high)) / 12.0]
  transfers between devices with their start and end apart: 8 -> 0, of which waited for: 2 -> 0; matrix products, arithmetic and copies ran while one was open for 42% -> 0% of each run, Pallas kernels for 0% -> 0%
where the time goes in v1:
time: 41.5 us; the launch traced here: 41.3 us
  Pallas kernels  39.1 us (94%)
  local copies, waits for them, and re-layouts  2.21 us (5%)
    pallas_call x1, Pallas kernels, local(): pl.pallas_call(functools.partial(kernel, (F, L, R, C, NLAT, NLON)), out_s...  39.1 us
    unnamed x1, local copies, waits for them, and re-layouts  2.21 us

profile of v1, /device:TPU:0, one launch (start us, length us, event | category | flops | bytes accessed | tf_op | source)
XLA Modules:
  0.0 41.3 jit_solution(14526992968630797302)
XLA Ops:
  0.0 39.1 %shard_map.73 = f32[16,120,128]{2,1,0:T(8,128)} custom-call(f32[16,120,128]{2,1,0:T(8,128)} %bitcast.4, f32[16,120,128]{2,1,0:T(8,128)} %bitcast.5, s32[480]{0:T(512)} %cut_ref.1, s32[480]{0:T(512)} %mask_ref.1, bf16[8,256,256]{2,1,0:T(8,128)(2,1)} %constant.6.clone.fwd_hbm, bf16[8,256,256]{2,1,0:T(8,128)(2,1)} %constant.7.clone.inv_hbm, ...), custom_call_target="tpu_custom_call" | custom-call | tf_op jit(solution)/shard_map/pallas_call | solution.py:345
  39.1 2.2 %copy.9 = f32[8,2,120,128]{3,2,1,0:T(8,128)} copy(f32[8,2,120,128]{3,2,1,0:T(8,128)} %bitcast.3) | data formatting | bytes 1966080

commit v2 on v1

--- a/solution.py
+++ b/solution.py
@@ -49,14 +49,16 @@
     return jnp.concatenate([high, low], axis=1)
 
 
-def kernel(dims, base_hbm, sec_hbm, cut_ref, mask_ref, fwd_hbm, inv_hbm, geo_hbm, out_ref,
-           pad, base, fwd, inv, geo, wts, msk, rowpack, halo, colpack, colrecv, comb, ul, ur, vf,
+def kernel(dims, sec_hbm, cut_ref, mask_ref, fwd_hbm, inv_hbm, geo_hbm, out_ref,
+           pad, fwd, inv, geo, wts, msk, rowpack, halo, colpack, colrecv, comb, ul, ur, vf,
            tend, msend, mrecv, zsend, zrecv, coef,
            lsem, hs_sem, hr_sem, ms_sem, mr_sem, zs_sem, zr_sem, cs_sem, cr_sem, fs_sem):
-    F, L, R, C, NLAT, NLON = dims
+    F, L, R, C, NLAT, NLON, H, RH = dims
     S = F * L
     G = NLON // 2
-    FG = F // G
+    U = F * H
+    UG = U // G
+    half = G // 2
     quarter = -(-NLAT // 4)
     band = lax.axis_index("lat")
     lon = lax.axis_index("lon")
@@ -67,10 +69,9 @@
 
     locals_ = [
         pltpu.make_async_copy(sec_hbm, pad.at[:, pl.ds(8, R), :], lsem.at[0]),
-        pltpu.make_async_copy(base_hbm, base, lsem.at[1]),
-        pltpu.make_async_copy(fwd_hbm.at[lon], fwd, lsem.at[2]),
-        pltpu.make_async_copy(inv_hbm.at[lon], inv, lsem.at[3]),
-        pltpu.make_async_copy(geo_hbm.at[band], geo, lsem.at[4]),
+        pltpu.make_async_copy(fwd_hbm.at[lon], fwd, lsem.at[1]),
+        pltpu.make_async_copy(inv_hbm.at[lon], inv, lsem.at[2]),
+        pltpu.make_async_copy(geo_hbm.at[band], geo, lsem.at[3]),
     ]
     for copy in locals_:
         copy.start()
@@ -84,8 +85,13 @@
     lo_slot = jnp.where(south, 0, 1)
     hi_slot = jnp.where(north, 1, 0)
 
+    side = g // half
+
     def peer(d):
-        return lax.rem(g + d, G)
+        i = lax.rem(d, half)
+        far = (1 - side) * half + lax.rem(g + i, half)
+        near = side * half + lax.rem(g + 1 + i, half)
+        return jnp.where(d < half, far, near)
 
     barrier = pltpu.get_barrier_semaphore()
     for target in ((band, left), (band, right), lo_dst, hi_dst):
@@ -93,7 +99,7 @@
 
     @pl.when(polar)
     def _():
-        for d in range(1, G):
+        for d in range(G - 1):
             pl.semaphore_signal(
                 barrier, inc=1, device_id=(band, peer(d) * 2 + core), device_id_type=MESH
             )
@@ -176,156 +182,179 @@
         return 7.0 * (pad[s, 7 : R + 15] + pad[s, 8 : R + 16]) - (pad[s, 6 : R + 14] + pad[s, 9 : R + 17])
 
     def winds(l):
-        ul[...], ur[...] = east(l)
-        vf[...] = northward(L + l) * geo[0]
-
-    def tendency(s):
+        ul[l], ur[l] = east(l)
+        vf[l] = northward(L + l) * geo[0]
+
+    def tendency(s, l):
         wl, wr = east(s)
-        fn = vf[...] * northward(s)
+        fn = vf[l] * northward(s)
         up = pltpu.roll(fn, R + 7, 0)
-        return ((ur[...] * wr - ul[...] * wl) + (up[:R] - fn[:R])) * geo[1, :R]
+        return ((ur[l] * wr - ul[l] * wl) + (up[:R] - fn[:R])) * geo[1, :R]
+
+    for l in range(L):
+        winds(l)
 
     @pl.when(jnp.logical_not(polar))
     def _():
-        def level(l, carry):
-            winds(l)
-
-            def field(f, inner):
-                s = f * L + l
-                out_ref[s] = base[s] + section_weight * tendency(s)
-                return inner
-
-            return lax.fori_loop(0, F, field, carry)
-
-        lax.fori_loop(0, L, level, 0)
+        def slab(s, carry):
+            out_ref[s] = section_weight * tendency(s, lax.rem(s, L))
+            return carry
+
+        lax.fori_loop(0, S, slab, 0)
 
     @pl.when(polar)
     def _():
         here, other = core, 1 - core
 
         def order(k):
-            return lax.rem((g + 1) * FG + k, F)
+            if H == 1:
+                return peer(k // UG) * UG + lax.rem(k, UG)
+            return lax.rem(g // (H // UG) + 1 + k, F)
+
+        def rows_of(h):
+            return h * RH, min(R, (h + 1) * RH)
 
         def partial_sums(f, l):
             s = f * L + l
-            t = tendency(s)
+            t = tendency(s, l)
             tend[s] = t
             both = jnp.dot(two_parts(t), fwd[...], preferred_element_type=jnp.float32)
             return both[:, :MODES] + both[:, MODES:]
 
         def to_mate(f):
-            return remote(msend.at[f], mrecv.at[f], ms_sem.at[f], mr_sem.at[f], (band, mate))
-
-        def to_owner(f):
-            slot = lax.rem(f, FG)
+            units = pl.ds(f * H, H)
             return remote(
-                zsend.at[f], zrecv.at[g * FG + slot], zs_sem.at[f], zr_sem.at[g * FG + slot],
-                (band, (f // FG) * 2 + core),
+                msend.at[units], mrecv.at[units], ms_sem.at[f], mr_sem.at[f], (band, mate)
             )
 
-        def to_peer(f, d):
-            at = here * F + f
+        def to_owner(u):
+            slot = g * UG + lax.rem(u, UG)
             return remote(
-                coef.at[at], coef.at[at], cs_sem.at[lax.rem(f, FG) * G + d], cr_sem.at[at],
+                zsend.at[u], zrecv.at[slot], zs_sem.at[u], zr_sem.at[slot],
+                (band, (u // UG) * 2 + core),
+            )
+
+        def to_peer(j, d):
+            at = here * U + g * UG + j
+            return remote(
+                coef.at[at], coef.at[at], cs_sem.at[j * G + d], cr_sem.at[at],
                 (band, peer(d) * 2 + core),
             )
 
-        def forward(f):
-            at = here * F + f
-            return remote(coef.at[at], coef.at[at], fs_sem.at[f], cr_sem.at[at], (band, mate))
+        def forward(u):
+            at = here * U + u
+            return remote(coef.at[at], coef.at[at], fs_sem.at[u], cr_sem.at[at], (band, mate))
 
         def arrived(at):
             return remote(coef.at[at], coef.at[at], fs_sem.at[0], cr_sem.at[at], (band, mate))
 
+        def store(ref, f, value):
+            for h in range(H):
+                first, last = rows_of(h)
+                ref[f * H + h, 0 : last - first] = value[first:last]
+
         def finish(f, l):
             s = f * L + l
-            both = jnp.dot(two_parts(coef[l * F + f]), inv[...], preferred_element_type=jnp.float32)
-            smooth = both[:, :C] + both[:, C:]
-            filtered = jnp.where(msk[...] == 1, smooth, tend[s])
-            out_ref[s] = base[s] + section_weight * filtered
-
-        winds(other)
+            for h in range(H):
+                first, last = rows_of(h)
+                c = coef[l * U + f * H + h]
+                both = jnp.dot(two_parts(c), inv[...], preferred_element_type=jnp.float32)
+                smooth = (both[:, :C] + both[:, C:])[: last - first]
+                out_ref[s, first:last] = section_weight * jnp.where(
+                    msk[first:last] == 1, smooth, tend[s, first:last]
+                )
+
+        def combine(f):
+            to_mate(f).wait_recv()
+            for h in range(H):
+                u = f * H + h
+                zsend[u] = zsend[u] + mrecv[u]
+
+                @pl.when(u // UG != g)
+                def _():
+                    to_owner(u).start()
+
+        if H > 1:
+            zsend[...] = jnp.zeros_like(zsend)
+            msend[...] = jnp.zeros_like(msend)
 
         def stage_a(k, carry):
             f = order(k)
-            msend[f] = partial_sums(f, other)
+            store(msend, f, partial_sums(f, other))
             to_mate(f).start()
+            store(zsend, f, partial_sums(f, here))
+
+            @pl.when(k > 0)
+            def _():
+                combine(order(k - 1))
+
             return carry
 
         lax.fori_loop(0, F, stage_a, 0)
-        winds(here)
-
-        def stage_b(k, carry):
-            f = order(k)
-            mine = partial_sums(f, here)
-            to_mate(f).wait_recv()
-            zsend[f] = mine + mrecv[f]
-
-            @pl.when(k < F - FG)
+        combine(order(F - 1))
+
+        def stage_c(j, carry):
+            u = g * UG + j
+            total = zsend[u]
+            for d in range(G - 1):
+                at = peer(d) * UG + j
+                remote(zsend.at[u], zrecv.at[at], zs_sem.at[u], zr_sem.at[at], (band, mate)).wait_recv()
+                total = total + zrecv[at]
+            first = pl.multiple_of(lax.rem(u, H) * RH, 8)
+            coef[here * U + u] = total * wts[pl.ds(first, RH), :]
+            for d in range(G - 1):
+                to_peer(j, d).start()
+            forward(u).start()
+            return carry
+
+        lax.fori_loop(0, UG, stage_c, 0)
+
+        def finish_other(f):
+            for h in range(H):
+                arrived(other * U + f * H + h).wait_recv()
+            finish(f, other)
+
+        def stage_d(k, carry):
+            f = order(F - 1 - k)
+            for h in range(H):
+                u = f * H + h
+
+                @pl.when(u // UG != g)
+                def _():
+                    arrived(here * U + u).wait_recv()
+                    forward(u).start()
+
+            finish(f, here)
+
+            @pl.when(k > 0)
             def _():
-                to_owner(f).start()
-
-            return carry
-
-        lax.fori_loop(0, F, stage_b, 0)
-
-        def stage_c(j, carry):
-            f = g * FG + j
-            total = zsend[f]
-            for d in range(1, G):
-                at = peer(d) * FG + j
-                remote(zsend.at[f], zrecv.at[at], zs_sem.at[f], zr_sem.at[at], (band, mate)).wait_recv()
-                total = total + zrecv[at]
-            coef[here * F + f] = total * wts[...]
-            for d in range(1, G):
-                to_peer(f, d).start()
-            forward(f).start()
-            return carry
-
-        lax.fori_loop(0, FG, stage_c, 0)
-
-        def own(j, carry):
-            finish(g * FG + j, here)
-            return carry
-
-        lax.fori_loop(0, FG, own, 0)
-
-        def stage_d(k, carry):
-            f = order(k)
-            arrived(here * F + f).wait_recv()
-            forward(f).start()
-            finish(f, here)
-            return carry
-
-        lax.fori_loop(0, F - FG, stage_d, 0)
-
-        def stage_e(k, carry):
-            f = lax.rem(g * FG + k, F)
-            arrived(other * F + f).wait_recv()
-            finish(f, other)
-            return carry
-
-        lax.fori_loop(0, F, stage_e, 0)
-
-        def drain(k, carry):
-            f = order(k)
+                finish_other(order(F - k))
+
+            return carry
+
+        lax.fori_loop(0, F, stage_d, 0)
+        finish_other(order(0))
+
+        def drain(f, carry):
             to_mate(f).wait_send()
-            forward(f).wait_send()
-
-            @pl.when(k < F - FG)
-            def _():
-                to_owner(f).wait_send()
+            for h in range(H):
+                u = f * H + h
+                forward(u).wait_send()
+
+                @pl.when(u // UG != g)
+                def _():
+                    to_owner(u).wait_send()
 
             return carry
 
         lax.fori_loop(0, F, drain, 0)
 
         def drain_peers(j, carry):
-            for d in range(1, G):
-                to_peer(g * FG + j, d).wait_send()
-            return carry
-
-        lax.fori_loop(0, FG, drain_peers, 0)
+            for d in range(G - 1):
+                to_peer(j, d).wait_send()
+            return carry
+
+        lax.fori_loop(0, UG, drain_peers, 0)
 
     for copy in halos:
         copy.wait_send()
@@ -335,51 +364,53 @@
     F, L, R, C = section_state.shape
     NLAT, NLON = lax.axis_size("lat"), lax.axis_size("lon")
     S, G = F * L, NLON // 2
-    FG = F // G
+    H = max(1, G // F)
+    RH = -(-R // (8 * H)) * 8
+    U = F * H
+    UG = U // G
     forward, inverse = basis_tables(NLON, C)
     geometry = geometry_table(NLAT, R, C)
     f32 = jnp.float32
     sem = pltpu.SemaphoreType.DMA
-    hbm = pl.BlockSpec(memory_space=pl.ANY)
+    hbm = pl.BlockSpec(memory_space=pltpu.HBM)
     smem = pl.BlockSpec(memory_space=pltpu.SMEM)
-    result = pl.pallas_call(
-        functools.partial(kernel, (F, L, R, C, NLAT, NLON)),
+    filtered = pl.pallas_call(
+        functools.partial(kernel, (F, L, R, C, NLAT, NLON, H, RH)),
         out_shape=jax.ShapeDtypeStruct((S, R, C), f32),
-        in_specs=[hbm, hbm, smem, smem, hbm, hbm, hbm],
+        in_specs=[hbm, smem, smem, hbm, hbm, hbm],
         out_specs=pl.BlockSpec(memory_space=pltpu.VMEM),
         scratch_shapes=[
             pltpu.VMEM((S, R + 24, C), f32),
-            pltpu.VMEM((S, R, C), f32),
             pltpu.VMEM((2 * C, 2 * MODES), jnp.bfloat16),
             pltpu.VMEM((2 * MODES, 2 * C), jnp.bfloat16),
             pltpu.VMEM((2, R + 8, C), f32),
-            pltpu.VMEM((R, MODES), f32),
+            pltpu.VMEM((H * RH, MODES), f32),
             pltpu.VMEM((R, C), jnp.int32),
             pltpu.VMEM((2, 2 * S, C), f32),
             pltpu.VMEM((2, 2 * S, C), f32),
             pltpu.VMEM((R, LANES), f32),
             pltpu.VMEM((2, R, LANES), f32),
             pltpu.VMEM((R, LANES), f32),
-            pltpu.VMEM((R, C), f32),
-            pltpu.VMEM((R, C), f32),
-            pltpu.VMEM((R + 8, C), f32),
+            pltpu.VMEM((L, R, C), f32),
+            pltpu.VMEM((L, R, C), f32),
+            pltpu.VMEM((L, R + 8, C), f32),
             pltpu.VMEM((S, R, C), f32),
-            pltpu.VMEM((F, R, MODES), f32),
-            pltpu.VMEM((F, R, MODES), f32),
-            pltpu.VMEM((F, R, MODES), f32),
-            pltpu.VMEM((F, R, MODES), f32),
-            pltpu.VMEM((S, R, MODES), f32),
-            sem((5,)), sem((4,)), sem((4,)), sem((F,)), sem((F,)), sem((F,)), sem((F,)),
-            sem((FG * G,)), sem((S,)), sem((F,)),
+            pltpu.VMEM((U, RH, MODES), f32),
+            pltpu.VMEM((U, RH, MODES), f32),
+            pltpu.VMEM((U, RH, MODES), f32),
+            pltpu.VMEM((U, RH, MODES), f32),
+            pltpu.VMEM((L * U, RH, MODES), f32),
+            sem((4,)), sem((4,)), sem((4,)), sem((F,)), sem((F,)), sem((U,)), sem((U,)),
+            sem((UG * G,)), sem((L * U,)), sem((U,)),
         ],
         compiler_params=pltpu.CompilerParams(
-            collective_id=0, has_side_effects=True, vmem_limit_bytes=56 * 1024 * 1024
+            collective_id=0, has_side_effects=True, vmem_limit_bytes=18 * S * R * C * 4
         ),
     )(
-        base_state.reshape(S, R, C), section_state.reshape(S, R, C), cutoff, filter_mask,
+        section_state.reshape(S, R, C), cutoff, filter_mask,
         jnp.asarray(forward), jnp.asarray(inverse), jnp.asarray(geometry),
     )
-    return result.reshape(F, L, R, C)
+    return base_state + filtered.reshape(F, L, R, C)
 
 
 def solution(mesh):

time: 41.5 us -> 44.1 us (1.063)
  local copies, waits for them, and re-layouts: 2.21 us -> 6.06 us
  Pallas kernels: 39.1 us -> 36.5 us
  other arithmetic: 0 us -> 1.04 us
    unnamed x1 -> x14, local copies, waits for them, and re-layouts: 2.21 us -> 6.06 us
    pallas_call x1, Pallas kernels: 39.1 us -> 36.5 us  [local(): pl.pallas_call(functools.partial(kernel, (F, L, R, C, NLAT, NLON, H, RH))...]
    add x0 -> x1, other arithmetic: none -> 1.04 us  [local(): return base_state + filtered.reshape(F, L, R, C)]
where the time goes in v2:
time: 44.1 us; the launch traced here: 43.7 us
  Pallas kernels  36.5 us (83%)
  local copies, waits for them, and re-layouts  6.06 us (14%)
  other arithmetic  1.04 us (2%)
    pallas_call x1, Pallas kernels, local(): pl.pallas_call(functools.partial(kernel, (F, L, R, C, NLAT, NLON, H, RH))...  36.5 us
    unnamed x14, local copies, waits for them, and re-layouts  6.06 us
    add x1, other arithmetic, local(): return base_state + filtered.reshape(F, L, R, C)  1.04 us

profile of v2, /device:TPU:0, one launch (start us, length us, event | category | flops | bytes accessed | tf_op | source)
XLA Modules:
  0.0 43.7 jit_solution(15799945965438189841)
XLA Ops:
  0.0 0.0 copy-start
  0.0 1.2 %copy-done = bf16[8,256,256]{2,1,0:T(8,128)(2,1)S(1)} copy-done((bf16[8,256,256]{2,1,0:T(8,128)(2,1)S(1)}, bf16[8,256,256]{2,1,0:T(8,128)(2,1)}, u32[]{:S(2)}) %copy-start) | copy-done | bytes 1048600
  1.2 0.0 copy-start.1
  1.2 1.2 %copy-done.1 = bf16[8,256,256]{2,1,0:T(8,128)(2,1)S(1)} copy-done((bf16[8,256,256]{2,1,0:T(8,128)(2,1)S(1)}, bf16[8,256,256]{2,1,0:T(8,128)(2,1)}, u32[]{:S(2)}) %copy-start.1) | copy-done | bytes 1048600
  2.5 0.0 copy-start.2
  2.5 1.2 %copy-done.2 = f32[8,2,120,128]{3,2,1,0:T(8,128)S(1)} copy-done((f32[8,2,120,128]{3,2,1,0:T(8,128)S(1)}, f32[8,2,120,128]{3,2,1,0:T(8,128)}, u32[]{:S(2)}) %copy-start.2) | copy-done | bytes 983064
  3.7 0.0 copy-start.3
  3.7 1.0 %copy-done.3 = f32[4,2,128,128]{3,2,1,0:T(8,128)S(1)} copy-done((f32[4,2,128,128]{3,2,1,0:T(8,128)S(1)}, f32[4,2,128,128]{3,2,1,0:T(8,128)}, u32[]{:S(2)}) %copy-start.3) | copy-done | bytes 524312
  4.7 0.0 copy-start.4
  4.7 0.7 %copy-done.4 = s32[480]{0:T(512)S(1)} copy-done((s32[480]{0:T(512)S(1)}, s32[480]{0:T(512)}, u32[]{:S(2)}) %copy-start.4) | copy-done | bytes 1944
  5.4 0.0 copy-start.5
  5.4 0.7 %copy-done.5 = s32[480]{0:T(512)S(1)} copy-done((s32[480]{0:T(512)S(1)}, s32[480]{0:T(512)}, u32[]{:S(2)}) %copy-start.5) | copy-done | bytes 1944
  6.1 0.0 copy-start.6
  6.1 36.5 %shard_map.73 = f32[16,120,128]{2,1,0:T(8,128)S(1)} custom-call(f32[16,120,128]{2,1,0:T(8,128)S(1)} %bitcast.3, s32[480]{0:T(512)S(1)} %copy-done.4, s32[480]{0:T(512)S(1)} %copy-done.5, bf16[8,256,256]{2,1,0:T(8,128)(2,1)S(1)} %copy-done.1, bf16[8,256,256]{2,1,0:T(8,128)(2,1)S(1)} %copy-done, f32[4,2,128,128]{3,2,1,0:T(8,128)S(1)} %copy-done.3), custom_call_target="tpu_custom_call" | custom-call | tf_op jit(solution)/shard_map/pallas_call | solution.py:377
  42.6 0.0 copy-done.6
  42.6 1.0 %add.3 = f32[8,2,120,128]{3,2,1,0:T(8,128)} add(f32[8,2,120,128]{3,2,1,0:T(8,128)S(1)} %copy-done.6, f32[8,2,120,128]{3,2,1,0:T(8,128)S(1)} %bitcast.2) | non-fusion elementwise | flops 245760 | bytes 2949120 | tf_op jit(solution)/shard_map/add | solution.py:413
Async XLA Ops:
  0.0 1.2 %copy-start = (bf16[8,256,256]{2,1,0:T(8,128)(2,1)S(1)}, bf16[8,256,256]{2,1,0:T(8,128)(2,1)}, u32[]{:S(2)}) copy-start(bf16[8,256,256]{2,1,0:T(8,128)(2,1)} %constant.7.clone.inv_hbm) | copy-start | bytes 3145732
  1.2 1.2 %copy-start.1 = (bf16[8,256,256]{2,1,0:T(8,128)(2,1)S(1)}, bf16[8,256,256]{2,1,0:T(8,128)(2,1)}, u32[]{:S(2)}) copy-start(bf16[8,256,256]{2,1,0:T(8,128)(2,1)} %constant.6.clone.fwd_hbm) | copy-start | bytes 3145732
  2.5 1.2 %copy-start.2 = (f32[8,2,120,128]{3,2,1,0:T(8,128)S(1)}, f32[8,2,120,128]{3,2,1,0:T(8,128)}, u32[]{:S(2)}) copy-start(f32[8,2,120,128]{3,2,1,0:T(8,128)} %param.8) | copy-start | bytes 2949124
  3.7 1.0 %copy-start.3 = (f32[4,2,128,128]{3,2,1,0:T(8,128)S(1)}, f32[4,2,128,128]{3,2,1,0:T(8,128)}, u32[]{:S(2)}) copy-start(f32[4,2,128,128]{3,2,1,0:T(8,128)} %constant.8.clone.geo_hbm) | copy-start | bytes 1572868
  4.7 0.7 %copy-start.4 = (s32[480]{0:T(512)S(1)}, s32[480]{0:T(512)}, u32[]{:S(2)}) copy-start(s32[480]{0:T(512)} %cut_ref.1) | copy-start | bytes 5764
  5.4 0.7 %copy-start.5 = (s32[480]{0:T(512)S(1)}, s32[480]{0:T(512)}, u32[]{:S(2)}) copy-start(s32[480]{0:T(512)} %mask_ref.1) | copy-start | bytes 5764
  6.1 36.5 %copy-start.6 = (f32[8,2,120,128]{3,2,1,0:T(8,128)S(1)}, f32[8,2,120,128]{3,2,1,0:T(8,128)}, u32[]{:S(2)}) copy-start(f32[8,2,120,128]{3,2,1,0:T(8,128)} %param.7) | copy-start | bytes 2949124

commit v3 on v2

--- a/solution.py
+++ b/solution.py
@@ -2,7 +2,6 @@
 
 import jax
 import jax.numpy as jnp
-import ml_dtypes
 import numpy as np
 from jax import lax
 from jax.experimental import pallas as pl
@@ -16,22 +15,11 @@
 MESH = pl.DeviceIdType.MESH
 
 
-def split_halves(table):
-    high = table.astype(ml_dtypes.bfloat16)
-    low = (table - high.astype(np.float64)).astype(ml_dtypes.bfloat16)
-    return high, low
-
-
-def basis_tables(lon_count, cols):
+def basis_table(lon_count, cols):
     total = lon_count * cols
     phase = (np.arange(total)[:, None] * np.arange(KMAX)[None, :]) % total * (2.0 * np.pi / total)
     basis = np.concatenate([np.cos(phase), np.sin(phase)], axis=1).reshape(lon_count, cols, MODES)
-    high, low = split_halves(basis)
-    wide = np.concatenate([high, low], axis=2)
-    forward = np.concatenate([wide, wide], axis=1)
-    tall = np.concatenate([high.transpose(0, 2, 1), low.transpose(0, 2, 1)], axis=2)
-    inverse = np.concatenate([tall, tall], axis=1)
-    return forward, inverse
+    return np.stack([basis, basis.transpose(0, 2, 1)], axis=1).astype(np.float32)
 
 
 def geometry_table(lat_count, rows, cols):
@@ -40,7 +28,7 @@
     face = np.where((faces == 0) | (faces >= total), 0.0, np.sin(np.pi * faces / total))
     cell = -1.0 / (144.0 * np.sin(np.pi * (np.minimum(faces, total - 1) + 0.5) / total))
     both = np.stack([face, cell], axis=1).astype(np.float32)
-    return np.ascontiguousarray(np.broadcast_to(both[..., None], both.shape + (cols,)))
+    return np.broadcast_to(both[..., None], both.shape + (cols,))
 
 
 def two_parts(value):
@@ -49,29 +37,32 @@
     return jnp.concatenate([high, low], axis=1)
 
 
-def kernel(dims, sec_hbm, cut_ref, mask_ref, fwd_hbm, inv_hbm, geo_hbm, out_ref,
-           pad, fwd, inv, geo, wts, msk, rowpack, halo, colpack, colrecv, comb, ul, ur, vf,
-           tend, msend, mrecv, zsend, zrecv, coef,
-           lsem, hs_sem, hr_sem, ms_sem, mr_sem, zs_sem, zr_sem, cs_sem, cr_sem, fs_sem):
+def kernel(dims, sec_hbm, cut_ref, mask_ref, table_hbm, out_ref,
+           pad, table, fwd, inv, geo, wts, msk, rowpack, halo, colpack, colrecv, comb, ul, ur, vf,
+           tend, msend, mrecv, zsend, zrecv, hrecv, coef,
+           lsem, hs_sem, hr_sem, ms_sem, mr_sem, zs_sem, zr_sem, xs_sem, xr_sem,
+           cs_sem, cr_sem, fs_sem):
     F, L, R, C, NLAT, NLON, H, RH = dims
     S = F * L
     G = NLON // 2
     U = F * H
-    UG = U // G
+    UG = U // (2 * G)
+    V = U // 2
     half = G // 2
-    quarter = -(-NLAT // 4)
+    quarter = NLAT // 4
     band = lax.axis_index("lat")
     lon = lax.axis_index("lon")
     core = lax.rem(lon, 2)
     g = lon // 2
     mate = g * 2 + 1 - core
-    polar = (band < quarter) | (band >= NLAT - quarter)
+    block = band // quarter
+    polar = (block == 0) | (block == 3)
+    partner = band + quarter * (1 - 2 * lax.rem(block, 2))
 
     locals_ = [
         pltpu.make_async_copy(sec_hbm, pad.at[:, pl.ds(8, R), :], lsem.at[0]),
-        pltpu.make_async_copy(fwd_hbm.at[lon], fwd, lsem.at[1]),
-        pltpu.make_async_copy(inv_hbm.at[lon], inv, lsem.at[2]),
-        pltpu.make_async_copy(geo_hbm.at[band], geo, lsem.at[3]),
+        pltpu.make_async_copy(table_hbm.at[lon], table, lsem.at[1]),
+        pltpu.make_async_copy(table_hbm.at[NLON + band], geo, lsem.at[2]),
     ]
     for copy in locals_:
         copy.start()
@@ -97,9 +88,11 @@
     for target in ((band, left), (band, right), lo_dst, hi_dst):
         pl.semaphore_signal(barrier, inc=1, device_id=target, device_id_type=MESH)
 
-    @pl.when(polar)
-    def _():
-        for d in range(G - 1):
+    for d in range(G):
+        pl.semaphore_signal(
+            barrier, inc=1, device_id=(partner, peer(d) * 2 + core), device_id_type=MESH
+        )
+        if d < G - 1:
             pl.semaphore_signal(
                 barrier, inc=1, device_id=(band, peer(d) * 2 + core), device_id_type=MESH
             )
@@ -117,7 +110,7 @@
         packed = jnp.where((lane >= 4 * s) & (lane < 4 * s + 4), shifted, packed)
     colpack[...] = packed
 
-    pl.semaphore_wait(barrier, jnp.where(polar, G + 3, 4))
+    pl.semaphore_wait(barrier, 2 * G + 3)
 
     def remote(src, dst, send, recv, target):
         return pltpu.make_async_remote_copy(
@@ -152,6 +145,13 @@
         remote(
             rowpack.at[slot], halo.at[slot], hs_sem.at[2 + slot], hr_sem.at[2 + slot], (band, right)
         ).wait_recv()
+
+    @pl.when(polar)
+    def _():
+        both = two_parts(table[0, :C, :MODES])
+        fwd[...] = jnp.concatenate([both, both], axis=0)
+        both = two_parts(table[1, :MODES])
+        inv[...] = jnp.concatenate([both, both], axis=0)
 
     comb[...] = jnp.where(lax.rem(lane, 4) < 2, colrecv[0], colrecv[1])
     index = lax.broadcasted_iota(jnp.int32, (2 * S, C), 0)
@@ -183,7 +183,7 @@
 
     def winds(l):
         ul[l], ur[l] = east(l)
-        vf[l] = northward(L + l) * geo[0]
+        vf[l] = northward(L + l) * geo[0, : R + 8]
 
     def tendency(s, l):
         wl, wr = east(s)
@@ -194,23 +194,97 @@
     for l in range(L):
         winds(l)
 
+    here, other = core, 1 - core
+
+    def order(k):
+        i = k // 2
+        if H == 1:
+            first = peer(i // UG) * UG + lax.rem(i, UG)
+        else:
+            first = lax.rem(g * UG // H + 1 + i, F // 2)
+        return first + (F // 2) * (1 - lax.rem(k, 2))
+
+    def to_helper(u):
+        v = u - V
+        return remote(
+            zsend.at[u], hrecv.at[v], xs_sem.at[v], xr_sem.at[v], (partner, lon)
+        )
+
+    def to_owner(ref, v):
+        slot = g * UG + lax.rem(v, UG)
+        return remote(
+            ref.at[v], zrecv.at[slot], zs_sem.at[v], zr_sem.at[slot],
+            (band, (v // UG) * 2 + core),
+        )
+
+    def gathered(ref, j):
+        total = ref[g * UG + j]
+        for d in range(G - 1):
+            at = peer(d) * UG + j
+            remote(
+                zsend.at[at], zrecv.at[at], zs_sem.at[at], zr_sem.at[at], (band, mate)
+            ).wait_recv()
+            total = total + zrecv[at]
+        return total
+
+    def publish(u, j, d, row):
+        at = here * U + u
+        return remote(
+            coef.at[at], coef.at[at], cs_sem.at[j * G + d], cr_sem.at[at],
+            (row, peer(d) * 2 + core),
+        )
+
     @pl.when(jnp.logical_not(polar))
     def _():
+        share = (3 * S) // (4 * (F // 2))
+
         def slab(s, carry):
             out_ref[s] = section_weight * tendency(s, lax.rem(s, L))
             return carry
 
-        lax.fori_loop(0, S, slab, 0)
+        def relay(i, carry):
+            lax.fori_loop(i * share, (i + 1) * share, slab, 0)
+            f = order(2 * i)
+            for h in range(H):
+                u = f * H + h
+                to_helper(u).wait_recv()
+
+                @pl.when((u - V) // UG != g)
+                def _():
+                    to_owner(hrecv, u - V).start()
+
+            return carry
+
+        lax.fori_loop(0, F // 2, relay, 0)
+        lax.fori_loop(share * (F // 2), S, slab, 0)
+
+        def sums(j, carry):
+            u = V + g * UG + j
+            coef[here * U + u] = gathered(hrecv, j)
+            for d in range(G):
+                publish(u, j, d, partner).start()
+            return carry
+
+        lax.fori_loop(0, UG, sums, 0)
+
+        def drain(v, carry):
+            @pl.when(v // UG != g)
+            def _():
+                to_owner(hrecv, v).wait_send()
+
+            return carry
+
+        lax.fori_loop(0, V, drain, 0)
+
+        def drain_sums(j, carry):
+            for d in range(G):
+                publish(V + g * UG + j, j, d, partner).wait_send()
+            return carry
+
+        lax.fori_loop(0, UG, drain_sums, 0)
 
     @pl.when(polar)
     def _():
-        here, other = core, 1 - core
-
-        def order(k):
-            if H == 1:
-                return peer(k // UG) * UG + lax.rem(k, UG)
-            return lax.rem(g // (H // UG) + 1 + k, F)
-
         def rows_of(h):
             return h * RH, min(R, (h + 1) * RH)
 
@@ -227,20 +301,6 @@
                 msend.at[units], mrecv.at[units], ms_sem.at[f], mr_sem.at[f], (band, mate)
             )
 
-        def to_owner(u):
-            slot = g * UG + lax.rem(u, UG)
-            return remote(
-                zsend.at[u], zrecv.at[slot], zs_sem.at[u], zr_sem.at[slot],
-                (band, (u // UG) * 2 + core),
-            )
-
-        def to_peer(j, d):
-            at = here * U + g * UG + j
-            return remote(
-                coef.at[at], coef.at[at], cs_sem.at[j * G + d], cr_sem.at[at],
-                (band, peer(d) * 2 + core),
-            )
-
         def forward(u):
             at = here * U + u
             return remote(coef.at[at], coef.at[at], fs_sem.at[u], cr_sem.at[at], (band, mate))
@@ -257,7 +317,7 @@
             s = f * L + l
             for h in range(H):
                 first, last = rows_of(h)
-                c = coef[l * U + f * H + h]
+                c = coef[l * U + f * H + h] * wts[h * RH : (h + 1) * RH]
                 both = jnp.dot(two_parts(c), inv[...], preferred_element_type=jnp.float32)
                 smooth = (both[:, :C] + both[:, C:])[: last - first]
                 out_ref[s, first:last] = section_weight * jnp.where(
@@ -270,9 +330,13 @@
                 u = f * H + h
                 zsend[u] = zsend[u] + mrecv[u]
 
-                @pl.when(u // UG != g)
-                def _():
-                    to_owner(u).start()
+                @pl.when(u >= V)
+                def _():
+                    to_helper(u).start()
+
+                @pl.when((u < V) & (u // UG != g))
+                def _():
+                    to_owner(zsend, u).start()
 
         if H > 1:
             zsend[...] = jnp.zeros_like(zsend)
@@ -295,15 +359,9 @@
 
         def stage_c(j, carry):
             u = g * UG + j
-            total = zsend[u]
+            coef[here * U + u] = gathered(zsend, j)
             for d in range(G - 1):
-                at = peer(d) * UG + j
-                remote(zsend.at[u], zrecv.at[at], zs_sem.at[u], zr_sem.at[at], (band, mate)).wait_recv()
-                total = total + zrecv[at]
-            first = pl.multiple_of(lax.rem(u, H) * RH, 8)
-            coef[here * U + u] = total * wts[pl.ds(first, RH), :]
-            for d in range(G - 1):
-                to_peer(j, d).start()
+                publish(u, j, d, band).start()
             forward(u).start()
             return carry
 
@@ -314,12 +372,15 @@
                 arrived(other * U + f * H + h).wait_recv()
             finish(f, other)
 
+        def back(k):
+            return order(jnp.where(k < F // 2, F - 1 - 2 * k, 2 * F - 2 - 2 * k))
+
         def stage_d(k, carry):
-            f = order(F - 1 - k)
+            f = back(k)
             for h in range(H):
                 u = f * H + h
 
-                @pl.when(u // UG != g)
+                @pl.when((u >= V) | (u // UG != g))
                 def _():
                     arrived(here * U + u).wait_recv()
                     forward(u).start()
@@ -328,12 +389,12 @@
 
             @pl.when(k > 0)
             def _():
-                finish_other(order(F - k))
+                finish_other(back(k - 1))
 
             return carry
 
         lax.fori_loop(0, F, stage_d, 0)
-        finish_other(order(0))
+        finish_other(back(F - 1))
 
         def drain(f, carry):
             to_mate(f).wait_send()
@@ -341,9 +402,13 @@
                 u = f * H + h
                 forward(u).wait_send()
 
-                @pl.when(u // UG != g)
-                def _():
-                    to_owner(u).wait_send()
+                @pl.when(u >= V)
+                def _():
+                    to_helper(u).wait_send()
+
+                @pl.when((u < V) & (u // UG != g))
+                def _():
+                    to_owner(zsend, u).wait_send()
 
             return carry
 
@@ -351,7 +416,7 @@
 
         def drain_peers(j, carry):
             for d in range(G - 1):
-                to_peer(j, d).wait_send()
+                publish(g * UG + j, j, d, band).wait_send()
             return carry
 
         lax.fori_loop(0, UG, drain_peers, 0)
@@ -364,12 +429,15 @@
     F, L, R, C = section_state.shape
     NLAT, NLON = lax.axis_size("lat"), lax.axis_size("lon")
     S, G = F * L, NLON // 2
-    H = max(1, G // F)
+    H = max(1, 2 * G // F)
     RH = -(-R // (8 * H)) * 8
     U = F * H
-    UG = U // G
-    forward, inverse = basis_tables(NLON, C)
-    geometry = geometry_table(NLAT, R, C)
+    UG = U // (2 * G)
+    bases, geometry = basis_table(NLON, C), geometry_table(NLAT, R, C)
+    tall = max(C, MODES, R + 8)
+    tables = np.zeros((NLON + NLAT, 2, tall, C), np.float32)
+    tables[:NLON, :, :C] = bases
+    tables[NLON:, :, : R + 8] = geometry
     f32 = jnp.float32
     sem = pltpu.SemaphoreType.DMA
     hbm = pl.BlockSpec(memory_space=pltpu.HBM)
@@ -377,13 +445,14 @@
     filtered = pl.pallas_call(
         functools.partial(kernel, (F, L, R, C, NLAT, NLON, H, RH)),
         out_shape=jax.ShapeDtypeStruct((S, R, C), f32),
-        in_specs=[hbm, smem, smem, hbm, hbm, hbm],
+        in_specs=[hbm, smem, smem, hbm],
         out_specs=pl.BlockSpec(memory_space=pltpu.VMEM),
         scratch_shapes=[
             pltpu.VMEM((S, R + 24, C), f32),
+            pltpu.VMEM((2, tall, C), f32),
             pltpu.VMEM((2 * C, 2 * MODES), jnp.bfloat16),
             pltpu.VMEM((2 * MODES, 2 * C), jnp.bfloat16),
-            pltpu.VMEM((2, R + 8, C), f32),
+            pltpu.VMEM((2, tall, C), f32),
             pltpu.VMEM((H * RH, MODES), f32),
             pltpu.VMEM((R, C), jnp.int32),
             pltpu.VMEM((2, 2 * S, C), f32),
@@ -398,17 +467,19 @@
             pltpu.VMEM((U, RH, MODES), f32),
             pltpu.VMEM((U, RH, MODES), f32),
             pltpu.VMEM((U, RH, MODES), f32),
-            pltpu.VMEM((U, RH, MODES), f32),
+            pltpu.VMEM((U // 2, RH, MODES), f32),
+            pltpu.VMEM((U // 2, RH, MODES), f32),
             pltpu.VMEM((L * U, RH, MODES), f32),
-            sem((4,)), sem((4,)), sem((4,)), sem((F,)), sem((F,)), sem((U,)), sem((U,)),
+            sem((4,)), sem((4,)), sem((4,)), sem((F,)), sem((F,)), sem((U // 2,)), sem((U // 2,)),
+            sem((U // 2,)), sem((U // 2,)),
             sem((UG * G,)), sem((L * U,)), sem((U,)),
         ],
         compiler_params=pltpu.CompilerParams(
-            collective_id=0, has_side_effects=True, vmem_limit_bytes=18 * S * R * C * 4
+            collective_id=0, has_side_effects=True, vmem_limit_bytes=55 * S * R * C * 4
         ),
     )(
         section_state.reshape(S, R, C), cutoff, filter_mask,
-        jnp.asarray(forward), jnp.asarray(inverse), jnp.asarray(geometry),
+        jnp.asarray(tables),
     )
     return base_state + filtered.reshape(F, L, R, C)
 

time: 44.1 us -> 34.8 us (0.79)
  Pallas kernels: 36.5 us -> 30.9 us
  local copies, waits for them, and re-layouts: 6.06 us -> 2.57 us
    pallas_call x1, Pallas kernels: 36.5 us -> 30.9 us  [local(): pl.pallas_call(functools.partial(kernel, (F, L, R, C, NLAT, NLON, H, RH))...]
    unnamed x14 -> x8, local copies, waits for them, and re-layouts: 6.06 us -> 2.57 us
where the time goes in v3:
time: 34.8 us; the launch traced here: 34.6 us
  Pallas kernels  30.9 us (89%)
  local copies, waits for them, and re-layouts  2.57 us (7%)
  other arithmetic  1.04 us (3%)
    pallas_call x1, Pallas kernels, local(): pl.pallas_call(functools.partial(kernel, (F, L, R, C, NLAT, NLON, H, RH))...  30.9 us
    unnamed x8, local copies, waits for them, and re-layouts  2.57 us
    add x1, other arithmetic, local(): return base_state + filtered.reshape(F, L, R, C)  1.04 us

profile of v3, /device:TPU:0, one launch (start us, length us, event | category | flops | bytes accessed | tf_op | source)
XLA Modules:
  0.0 34.6 jit_solution(4553180638746314318)
XLA Ops:
  0.0 0.0 copy-start
  0.0 1.2 %copy-done = f32[8,2,120,128]{3,2,1,0:T(8,128)S(1)} copy-done((f32[8,2,120,128]{3,2,1,0:T(8,128)S(1)}, f32[8,2,120,128]{3,2,1,0:T(8,128)}, u32[]{:S(2)}) %copy-start) | copy-done | bytes 983064
  1.2 0.0 copy-start.1
  1.2 0.7 %copy-done.1 = s32[480]{0:T(512)S(1)} copy-done((s32[480]{0:T(512)S(1)}, s32[480]{0:T(512)}, u32[]{:S(2)}) %copy-start.1) | copy-done | bytes 1944
  1.9 0.0 copy-start.2
  1.9 0.7 %copy-done.2 = s32[480]{0:T(512)S(1)} copy-done((s32[480]{0:T(512)S(1)}, s32[480]{0:T(512)}, u32[]{:S(2)}) %copy-start.2) | copy-done | bytes 1944
  2.6 0.0 copy-start.3
  2.6 30.9 %shard_map.55 = f32[16,120,128]{2,1,0:T(8,128)S(1)} custom-call(f32[16,120,128]{2,1,0:T(8,128)S(1)} %bitcast.3, s32[480]{0:T(512)S(1)} %copy-done.1, s32[480]{0:T(512)S(1)} %copy-done.2, f32[12,2,128,128]{3,2,1,0:T(8,128)} %constant.2.clone.table_hbm), custom_call_target="tpu_custom_call" | custom-call | tf_op jit(solution)/shard_map/pallas_call | solution.py:445
  33.5 0.0 copy-done.3
  33.5 1.0 %add.3 = f32[8,2,120,128]{3,2,1,0:T(8,128)} add(f32[8,2,120,128]{3,2,1,0:T(8,128)S(1)} %copy-done.3, f32[8,2,120,128]{3,2,1,0:T(8,128)S(1)} %bitcast.2) | non-fusion elementwise | flops 245760 | bytes 2949120 | tf_op jit(solution)/shard_map/add | solution.py:484
Async XLA Ops:
  0.0 1.2 %copy-start = (f32[8,2,120,128]{3,2,1,0:T(8,128)S(1)}, f32[8,2,120,128]{3,2,1,0:T(8,128)}, u32[]{:S(2)}) copy-start(f32[8,2,120,128]{3,2,1,0:T(8,128)} %param.6) | copy-start | bytes 2949124
  1.2 0.7 %copy-start.1 = (s32[480]{0:T(512)S(1)}, s32[480]{0:T(512)}, u32[]{:S(2)}) copy-start(s32[480]{0:T(512)} %cut_ref.1) | copy-start | bytes 5764
  1.9 0.7 %copy-start.2 = (s32[480]{0:T(512)S(1)}, s32[480]{0:T(512)}, u32[]{:S(2)}) copy-start(s32[480]{0:T(512)} %mask_ref.1) | copy-start | bytes 5764
  2.6 30.9 %copy-start.3 = (f32[8,2,120,128]{3,2,1,0:T(8,128)S(1)}, f32[8,2,120,128]{3,2,1,0:T(8,128)}, u32[]{:S(2)}) copy-start(f32[8,2,120,128]{3,2,1,0:T(8,128)} %param.5) | copy-start | bytes 2949124

commit v4 on v3

--- a/solution.py
+++ b/solution.py
@@ -37,7 +37,7 @@
     return jnp.concatenate([high, low], axis=1)
 
 
-def kernel(dims, sec_hbm, cut_ref, mask_ref, table_hbm, out_ref,
+def kernel(dims, sec_hbm, code_ref, table_hbm, out_ref,
            pad, table, fwd, inv, geo, wts, msk, rowpack, halo, colpack, colrecv, comb, ul, ur, vf,
            tend, msend, mrecv, zsend, zrecv, hrecv, coef,
            lsem, hs_sem, hr_sem, ms_sem, mr_sem, zs_sem, zr_sem, xs_sem, xr_sem,
@@ -132,8 +132,9 @@
         scale = jnp.where(mode == 0, 1.0 / (C * NLON), 2.0 / (C * NLON)).astype(jnp.float32)
 
         def row(r, carry):
-            wts[pl.ds(r, 1), :] = jnp.where(mode < cut_ref[band * R + r], scale, 0.0)
-            msk[pl.ds(r, 1), :] = jnp.broadcast_to(mask_ref[band * R + r], (1, C))
+            code = code_ref[band * R + r]
+            wts[pl.ds(r, 1), :] = jnp.where(mode < code // 2, scale, 0.0)
+            msk[pl.ds(r, 1), :] = jnp.broadcast_to(lax.rem(code, 2), (1, C))
             return carry
 
         lax.fori_loop(0, R, row, 0)
@@ -198,8 +199,8 @@
 
     def order(k):
         i = k // 2
-        if H == 1:
-            first = peer(i // UG) * UG + lax.rem(i, UG)
+        if UG % H == 0:
+            first = peer(i // (UG // H)) * (UG // H) + lax.rem(i, UG // H)
         else:
             first = lax.rem(g * UG // H + 1 + i, F // 2)
         return first + (F // 2) * (1 - lax.rem(k, 2))
@@ -236,7 +237,7 @@
 
     @pl.when(jnp.logical_not(polar))
     def _():
-        share = (3 * S) // (4 * (F // 2))
+        share = S // (F // 2)
 
         def slab(s, carry):
             out_ref[s] = section_weight * tendency(s, lax.rem(s, L))
@@ -338,7 +339,7 @@
                 def _():
                     to_owner(zsend, u).start()
 
-        if H > 1:
+        if H * RH > R:
             zsend[...] = jnp.zeros_like(zsend)
             msend[...] = jnp.zeros_like(msend)
 
@@ -445,7 +446,7 @@
     filtered = pl.pallas_call(
         functools.partial(kernel, (F, L, R, C, NLAT, NLON, H, RH)),
         out_shape=jax.ShapeDtypeStruct((S, R, C), f32),
-        in_specs=[hbm, smem, smem, hbm],
+        in_specs=[hbm, smem, hbm],
         out_specs=pl.BlockSpec(memory_space=pltpu.VMEM),
         scratch_shapes=[
             pltpu.VMEM((S, R + 24, C), f32),
@@ -475,10 +476,11 @@
             sem((UG * G,)), sem((L * U,)), sem((U,)),
         ],
         compiler_params=pltpu.CompilerParams(
-            collective_id=0, has_side_effects=True, vmem_limit_bytes=55 * S * R * C * 4
+            collective_id=0, has_side_effects=True, vmem_limit_bytes=int(56.4 * S * R * C * 4)
         ),
     )(
-        section_state.reshape(S, R, C), cutoff, filter_mask,
+        section_state.reshape(S, R, C),
+        2 * cutoff + jnp.where(filter_mask == 1, 1, 0),
         jnp.asarray(tables),
     )
     return base_state + filtered.reshape(F, L, R, C)

time: 34.8 us -> 33.1 us (0.951)
  local copies, waits for them, and re-layouts: 2.57 us -> 0.01 us
  other arithmetic: 1.04 us -> 1.75 us
    unnamed x8 -> x2, local copies, waits for them, and re-layouts: 2.57 us -> 0.01 us
    add x0 -> x1, other arithmetic: none -> 0.7 us  [local(): 2 * cutoff + jnp.where(filter_mask == 1, 1, 0)]
where the time goes in v4:
time: 33.1 us; the launch traced here: 32.6 us
  Pallas kernels  30.8 us (93%)
  other arithmetic  1.75 us (5%)
    pallas_call x1, Pallas kernels, local(): pl.pallas_call(functools.partial(kernel, (F, L, R, C, NLAT, NLON, H, RH))...  30.8 us
    add x1, other arithmetic, local(): return base_state + filtered.reshape(F, L, R, C)  1.04 us
    add x1, other arithmetic, local(): 2 * cutoff + jnp.where(filter_mask == 1, 1, 0)  0.7 us

profile of v4, /device:TPU:0, one launch (start us, length us, event | category | flops | bytes accessed | tf_op | source)
XLA Modules:
  0.0 32.6 jit_solution(14728653993579532959)
XLA Ops:
  0.0 0.7 %select_add_fusion.code_ref = s32[480]{0:T(512)S(1)} fusion(s32[480]{0:T(512)} %param.7, s32[480]{0:T(512)} %param.8), kind=kLoop, calls=%fused_computation | loop fusion | flops 1920 | bytes 5760 | tf_op jit(solution)/shard_map/add | solution.py:483
  0.7 0.0 copy-start
  0.7 30.8 %shard_map.55 = f32[16,120,128]{2,1,0:T(8,128)S(1)} custom-call(f32[16,120,128]{2,1,0:T(8,128)} %bitcast.3, s32[480]{0:T(512)S(1)} %select_add_fusion.code_ref, f32[12,2,128,128]{3,2,1,0:T(8,128)} %constant.3.clone.table_hbm), custom_call_target="tpu_custom_call" | custom-call | tf_op jit(solution)/shard_map/pallas_call | solution.py:446
  31.5 0.0 copy-done
  31.6 1.0 %add.7 = f32[8,2,120,128]{3,2,1,0:T(8,128)} add(f32[8,2,120,128]{3,2,1,0:T(8,128)S(1)} %copy-done, f32[8,2,120,128]{3,2,1,0:T(8,128)S(1)} %bitcast.2) | non-fusion elementwise | flops 245760 | bytes 2949120 | tf_op jit(solution)/shard_map/add | solution.py:486
Async XLA Ops:
  0.7 30.8 %copy-start = (f32[8,2,120,128]{3,2,1,0:T(8,128)S(1)}, f32[8,2,120,128]{3,2,1,0:T(8,128)}, u32[]{:S(2)}) copy-start(f32[8,2,120,128]{3,2,1,0:T(8,128)} %param.5) | copy-start | bytes 2949124
